TPU v7x, 128 devices: a whole 4x4x4 slice. The times are simulated.
128 devices in a mesh: ctx: 8 (over y, x_lo), dp: 16 (over z, x_hi, core).
Axes of the slice: x: 4 (x_hi: 2, x_lo: 2; x = x_hi * 2 + x_lo), y: 4, z: 4, core: 2. Of those that a mesh axis runs over, the one named last changes fastest.
Arguments:
- layer_input: bfloat16 [16, 4096, 4096], P('dp', 'ctx'), may hold values from -8 to 8
- grad_out: bfloat16 [16, 4096, 4096], P('dp', 'ctx'), may hold values from -0.25 to 0.25
- w_in: bfloat16 [4096, 1024], P(('ctx', 'dp')), may hold values from -0.09375 to 0.09375
- w_out_t: bfloat16 [4096, 256], P(('ctx', 'dp')), may hold values from -0.375 to 0.375
- decay_rate: float32 [128], replicated, may hold values from 2.4414063e-05 to 0.0625
Outputs:
- grad_input: bfloat16 [16, 4096, 4096], P('dp', 'ctx')
- grad_w_in: float32 [4096, 1024], P(('ctx', 'dp'))
- grad_w_out_t: float32 [4096, 256], P(('ctx', 'dp'))
All inputs are finite; a program needn't handle non-finite values.
Results may differ from a plain program's by a relative error of at most 0.02.
Values may be sent and summed in bfloat16 or wider, within the bound.
A program may use at most 192 MiB of HBM per device.

v0:
```python
import math

import jax
import jax.numpy as jnp
from jax import lax
from jax.sharding import PartitionSpec as P

BLOCK = 256


EPSILON = 1e-06
HIGHEST = lax.Precision.HIGHEST


def entering(array, axis, combine, identity, reverse):
    devices, here = (lax.axis_size(axis), lax.axis_index(axis))
    everything = jax.tree.map(
        lambda part, kind: lax.all_gather(part.astype(kind), axis),
        array,
        (jnp.bfloat16, jnp.bfloat16),
    )
    start = jax.tree.map(
        lambda part, zero: jnp.broadcast_to(jnp.asarray(zero, part.dtype), part.shape),
        array,
        identity,
    )

    def step(k, before):
        at = devices - 1 - k if reverse else k
        reached = at > here if reverse else at < here
        new = combine(
            before, jax.tree.map(lambda part, own: part[at].astype(own.dtype), everything, array)
        )
        return jax.tree.map(lambda a, b: jnp.where(reached, a, b), new, before)

    return lax.fori_loop(0, devices, step, start)


def rope_tables(first_row, row_count, half_width):
    position = (first_row + jnp.arange(row_count)).astype(jnp.float32)
    spacing = jnp.exp(
        jnp.arange(half_width).astype(jnp.float32) * (-math.log(10000.0) / half_width)
    )
    angles = position[:, None] * spacing[None, :]
    return (jnp.cos(angles), jnp.sin(angles))


def rotate(values_in, cosine, sine):
    half_width = cosine.shape[1]
    leading = values_in[:, :half_width].astype(jnp.float32)
    trailing = values_in[:, half_width:].astype(jnp.float32)
    return jnp.concatenate(
        [leading * cosine - trailing * sine, leading * sine + trailing * cosine], axis=1
    )


def unrotate(values_in, cosine, sine):
    half_width = cosine.shape[1]
    leading = values_in[:, :half_width]
    trailing = values_in[:, half_width:]
    return jnp.concatenate(
        [leading * cosine + trailing * sine, trailing * cosine - leading * sine], axis=1
    )


def gate_norm(retained, gate_pre, grad_hidden):
    mean_sq = jnp.mean(retained * retained, axis=1, keepdims=True)
    inverse = lax.rsqrt(mean_sq + EPSILON)
    normed = retained * inverse
    gate_f = gate_pre.astype(jnp.float32)
    sigmoid_g = jax.nn.sigmoid(gate_f)
    hidden = (gate_f * sigmoid_g * normed).astype(jnp.bfloat16)
    grad_normed = grad_hidden * gate_f * sigmoid_g
    grad_gate = grad_hidden * normed * sigmoid_g * (1.0 + gate_f * (1.0 - sigmoid_g))
    grad_ret = (
        inverse * (grad_normed - normed * jnp.mean(grad_normed * normed, axis=1, keepdims=True))
    ).astype(jnp.bfloat16)
    return (hidden, grad_gate, grad_ret)


def chain_combine(earlier, later):
    return (later[1][:, None] * earlier[0] + later[0], earlier[1] * later[1])


def contract_rows(left, right):
    return lax.dot_general(left, right, (((0,), (0,)), ((), ())), precision=HIGHEST)


def on_device(layer_input, grad_out, w_in, w_out_t, decay_rate):
    tokens = layer_input[0]
    upstream = grad_out[0]
    seq_rows = tokens.shape[0]
    head = w_out_t.shape[1]
    half_width = head // 2
    rates = jnp.concatenate([decay_rate, decay_rate])
    shard_pos = lax.axis_index("ctx")
    cosine, sine = rope_tables(shard_pos * seq_rows, seq_rows, half_width)
    w_in_all, w_out_all = (
        lax.all_gather(w_in, ("ctx", "dp"), axis=0, tiled=True),
        lax.all_gather(w_out_t, ("ctx", "dp"), axis=0, tiled=True),
    )
    projected = jnp.dot(tokens, w_in_all, preferred_element_type=jnp.float32)
    grad_hidden = jnp.dot(upstream, w_out_all, preferred_element_type=jnp.float32)
    proj = projected.astype(jnp.bfloat16)
    queries = proj[:, :head]
    keys_in = proj[:, head : 2 * head]
    values_in = proj[:, 2 * head : 3 * head]
    gate_pre = proj[:, 3 * head :]
    q_rot = rotate(queries, cosine, sine).astype(jnp.bfloat16)
    k_rot = rotate(keys_in, cosine, sine).astype(jnp.bfloat16)
    query_full = q_rot.astype(jnp.float32)
    key_full = k_rot.astype(jnp.float32)
    value_full = values_in.astype(jnp.float32)
    shard_offsets = jnp.arange(seq_rows).astype(jnp.float32)[:, None]
    zero_state = jnp.zeros((head, head), jnp.float32)
    shard_decay = jnp.exp(-seq_rows * rates)
    state_local = contract_rows(
        key_full * jnp.exp(-(seq_rows - 1.0 - shard_offsets) * rates[None, :]), value_full
    )
    state_in = entering(
        (state_local, shard_decay),
        "ctx",
        chain_combine,
        (zero_state, jnp.ones((head,), jnp.float32)),
        False,
    )[0]
    offsets = jnp.arange(BLOCK).astype(jnp.float32)[:, None]
    center = 0.5 * BLOCK
    query_scale = jnp.exp(-(offsets - center) * rates[None, :])
    key_scale = jnp.exp(-(center - offsets) * rates[None, :])
    enter_state = jnp.exp(-(offsets + 1.0) * rates[None, :])
    fade_out = jnp.exp(-(BLOCK - 1.0 - offsets) * rates[None, :])
    leave_state = jnp.exp(-(BLOCK - offsets) * rates[None, :])
    from_start = jnp.exp(-offsets * rates[None, :])
    block_decay = jnp.exp(-BLOCK * rates)
    causal = offsets >= offsets.T
    blocks = seq_rows // BLOCK

    def block_scores(query_blk, key_blk):
        query_scaled = query_blk * query_scale
        key_scaled = key_blk * key_scale
        scores = jnp.where(causal, jnp.dot(query_scaled, key_scaled.T, precision=HIGHEST), 0.0)
        return (scores, query_scaled, key_scaled)

    def forward_step(state, block):
        query_blk, key_blk, value_blk = block
        scores, _, _ = block_scores(query_blk, key_blk)
        retained_blk = jnp.dot(scores, value_blk, precision=HIGHEST) + jnp.dot(
            query_blk * enter_state, state, precision=HIGHEST
        )
        new_state = block_decay[:, None] * state + contract_rows(key_blk * fade_out, value_blk)
        return (new_state, (retained_blk, state))

    query_blocks = query_full.reshape(blocks, BLOCK, head)
    key_blocks = key_full.reshape(blocks, BLOCK, head)
    value_blocks = value_full.reshape(blocks, BLOCK, head)
    _, (retained_blocks, state_blocks) = lax.scan(
        forward_step, state_in, (query_blocks, key_blocks, value_blocks)
    )
    retained = retained_blocks.reshape(seq_rows, head)
    hidden, grad_gate, grad_ret = gate_norm(retained, gate_pre, grad_hidden)
    grad_full = grad_ret.astype(jnp.float32)
    grad_local = contract_rows(query_full * jnp.exp(-shard_offsets * rates[None, :]), grad_full)
    grad_in_state = entering(
        (grad_local, shard_decay),
        "ctx",
        chain_combine,
        (zero_state, jnp.ones((head,), jnp.float32)),
        True,
    )[0]

    def backward_step(grad_state, block):
        query_blk, key_blk, value_blk, grad_blk, state = block
        scores, query_scaled, key_scaled = block_scores(query_blk, key_blk)
        score_grad = jnp.where(causal, jnp.dot(grad_blk, value_blk.T, precision=HIGHEST), 0.0)
        grad_query = (
            jnp.dot(score_grad, key_scaled, precision=HIGHEST) * query_scale
            + jnp.dot(grad_blk, state.T, precision=HIGHEST) * enter_state
        )
        grad_key = (
            jnp.dot(score_grad.T, query_scaled, precision=HIGHEST) * key_scale
            + jnp.dot(value_blk, grad_state.T, precision=HIGHEST) * leave_state
        )
        grad_value = jnp.dot(scores.T, grad_blk, precision=HIGHEST) + jnp.dot(
            key_blk * leave_state, grad_state, precision=HIGHEST
        )
        new_grad_state = block_decay[:, None] * grad_state + contract_rows(
            query_blk * from_start, grad_blk
        )
        return (new_grad_state, (grad_query, grad_key, grad_value))

    grad_blocks = grad_full.reshape(blocks, BLOCK, head)
    _, (grad_q_blocks, grad_k_blocks, grad_v_blocks) = lax.scan(
        backward_step,
        grad_in_state,
        (query_blocks, key_blocks, value_blocks, grad_blocks, state_blocks),
        reverse=True,
    )
    grad_qrot = grad_q_blocks.reshape(seq_rows, head)
    grad_krot = grad_k_blocks.reshape(seq_rows, head)
    grad_values = grad_v_blocks.reshape(seq_rows, head)
    grad_proj = jnp.concatenate(
        [
            unrotate(grad_qrot, cosine, sine),
            unrotate(grad_krot, cosine, sine),
            grad_values,
            grad_gate,
        ],
        axis=1,
    ).astype(jnp.bfloat16)
    grad_tokens = lax.dot_general(
        grad_proj, w_in_all, (((1,), (1,)), ((), ())), preferred_element_type=jnp.float32
    ).astype(jnp.bfloat16)
    term_in = lax.dot_general(
        tokens, grad_proj, (((0,), (0,)), ((), ())), preferred_element_type=jnp.float32
    )
    term_out = lax.dot_general(
        upstream, hidden, (((0,), (0,)), ((), ())), preferred_element_type=jnp.float32
    )
    reduced = lax.psum_scatter(
        jnp.concatenate([term_in, term_out], axis=1), ("ctx", "dp"), scatter_dimension=0, tiled=True
    )
    return (grad_tokens[None], reduced[:, : 4 * head], reduced[:, 4 * head :])


def solution(mesh):
    placed = (
        P("dp", "ctx", None),
        P("dp", "ctx", None),
        P(("ctx", "dp"), None),
        P(("ctx", "dp"), None),
        P(),
    )
    return jax.shard_map(
        on_device,
        mesh=mesh,
        in_specs=placed,
        out_specs=(P("dp", "ctx", None), P(("ctx", "dp"), None), P(("ctx", "dp"), None)),
        check_vma=False,
    )
```

profile of v0, /device:TPU:0, one launch (start us, length us, event | category | flops | bytes accessed | tf_op | source)
XLA Modules:
  0.0 1272.6 jit_solution(595596509725653759)
XLA Ops:
  9.4 206.1 %all-gather.8.cloned.1.call-done = bf16[4096,1024]{1,0:T(8,128)(2,1)} async-done(((bf16[32,1024]{1,0:T(8,128)(2,1)}), bf16[4096,1024]{1,0:T(8,128)(2,1)}) %all-gather.8.cloned.1.call-update) | async-done | bytes 8388624 | tf_op jit(solution)/shard_map/all_gather | solution.py:99
  215.5 9.1 fusion.118
  230.5 17.2 %all-gather.2 = bf16[8,1,256]{2,1,0:T(2,128)(2,1)S(1)} all-gather(bf16[1,1,256]{2,1,0:T(2,128)(2,1)S(1)} %fusion.186), channel_id=1, replica_groups=mesh['ctx'=8,'dp'=16] {'ctx'}, dimensions={0}, use_global_device_ids=true | all-gather | bytes 4608 | tf_op jit(solution)/shard_map/all_gather | solution.py:18
  247.8 18.3 %all-gather.12.cloned.1.call-done = bf16[2048,256]{1,0:T(8,128)(2,1)} async-done(((bf16[256,256]{1,0:T(8,128)(2,1)}), bf16[2048,256]{1,0:T(8,128)(2,1)}) %all-gather.12.cloned.1.call-update) | async-done | bytes 1048592 | tf_op jit(solution)/shard_map/all_gather | solution.py:18
  266.2 8.6 while.69
  275.4 7.0 while.71
  277.5 1.4 convolution_add_fusion.6
  281.0 1.4 convolution_add_fusion.6
  282.6 179.5 %all-gather.10.cloned.1.call-done = bf16[4096,256]{1,0:T(8,128)(2,1)} async-done(((bf16[32,256]{1,0:T(8,128)(2,1)}), bf16[4096,256]{1,0:T(8,128)(2,1)}) %all-gather.10.cloned.1.call-update) | async-done | bytes 2097168 | tf_op jit(solution)/shard_map/all_gather | solution.py:100
  462.0 4.2 multiply_reduce_fusion
  466.2 2.1 fusion.127
  470.6 5.5 convolution_bitcast_fusion.1
  476.1 32.5 %all-gather.14.cloned.1.call-done = bf16[2048,256]{1,0:T(8,128)(2,1)} async-done(((bf16[256,256]{1,0:T(8,128)(2,1)}), bf16[2048,256]{1,0:T(8,128)(2,1)}) %all-gather.14.cloned.1.call-update) | async-done | bytes 1048592 | tf_op jit(solution)/shard_map/all_gather | solution.py:18
  508.6 14.0 %while.70 = (s32[]{:T(128)}, f32[256,256]{1,0:T(8,128)S(1)}, s32[]{:T(128)}, bf16[8,256]{1,0:T(8,128)(2,1)}, bf16[8,256,256]{2,1,0:T(8,128)(2,1)}, /*index=5*/s32[]{:T(128)}, s32[]{:T(128)}, s32[]{:T(128)}, s32[]{:T(128)}) while((s32[]{:T(128)}, f32[256,256]{1,0:T(8,128)S(1)}, s32[]{:T(128)}, bf16[8,256]{1,0:T(8,128)(2,1)}, ...), condition=%wide.region_7.8_spmd.clone, body=%wide.region_6.7_spmd.clone.sunk | while | flops 327944 | bytes 658095 | solution.py:36
  523.5 11.0 while.72
  534.5 2.1 fusion.183
  536.6 2.1 fusion.182
  543.1 6.6 convolution_bitcast_fusion
  549.7 9.5 pad_maximum_fusion
  559.2 22.5 %copy.14 = f32[4096,1280]{1,0:T(8,128)} copy(f32[4096,1280]{0,1:T(8,128)} %pad_maximum_fusion) | data formatting | bytes 41943040
  581.8 9.5 fusion.111
  591.3 671.9 %reduce-scatter.4.cloned.1.call-done = f32[32,1280]{1,0:T(8,128)} async-done(((f32[4096,1280]{1,0:T(8,128)}), f32[32,1280]{1,0:T(8,128)}) %reduce-scatter.4.cloned.1.call-update) | async-done | bytes 163856
  1263.2 1.4 slice.65
  1264.5 1.6 slice.64
  (139 shorter events, 53.2 us)
Async XLA Ops:
  7.2 208.3 %all-gather.8.cloned.1.call-start = ((), (), s32[]{:S(2)}) async-start(), calls=%async_computation.1 | async-start | bytes 8454144 | tf_op jit(solution)/shard_map/all_gather | solution.py:99
  7.9 258.3 %all-gather.12.cloned.1.call-start = ((), (), s32[]{:S(2)}) async-start(), calls=%async_computation.3 | async-start | bytes 1179648 | tf_op jit(solution)/shard_map/all_gather | solution.py:18
  8.0 216.7 %copy-start.11 = (f32[128]{0:T(128)}, f32[128]{0:T(128)S(1)}, u32[]{:S(2)}) copy-start(f32[128]{0:T(128)S(1)} %multiply_exponential_fusion.9) | copy-start | bytes 1540
  9.3 215.3 %copy-start.8 = (f32[512]{0:T(512)}, f32[512]{0:T(512)S(1)}, u32[]{:S(2)}) copy-start(f32[512]{0:T(512)S(1)} %add_convert_fusion) | copy-start | bytes 6148
  9.3 221.1 %copy-start.14 = (f32[128]{0:T(128)S(1)}, f32[128]{0:T(128)}, u32[]{:S(2)}) copy-start(f32[128]{0:T(128)} %param.17) | copy-start | bytes 1540
  224.7 41.5 %copy-start.3 = (bf16[512,1024]{1,0:T(8,128)(2,1)}, bf16[512,1024]{1,0:T(8,128)(2,1)S(1)}, u32[]{:S(2)}) copy-start(bf16[512,1024]{1,0:T(8,128)(2,1)S(1)} %fusion.118) | copy-start | bytes 3145732
  226.0 21.8 %copy-start.4 = (bf16[512,128]{1,0:T(8,128)(2,1)}, bf16[512,128]{1,0:T(8,128)(2,1)S(1)}, u32[]{:S(2)}) copy-start(bf16[512,128]{1,0:T(8,128)(2,1)S(1)} %get-tuple-element.1000) | copy-start | bytes 393220
  227.3 234.7 %all-gather.10.cloned.1.call-start = ((), (), s32[]{:S(2)}) async-start(), calls=%async_computation.2 | async-start | bytes 2113536 | tf_op jit(solution)/shard_map/all_gather | solution.py:100
  228.1 280.5 %all-gather.14.cloned.1.call-start = ((), (), s32[]{:S(2)}) async-start(), calls=%async_computation.4 | async-start | bytes 1179648 | tf_op jit(solution)/shard_map/all_gather | solution.py:18
  274.8 0.6 copy-start.10
  462.0 6.3 copy-start.5
  462.0 6.3 copy-start.13
  469.7 793.4 %reduce-scatter.4.cloned.1.call-start = ((), (), s32[]{:S(2)}) async-start(), calls=%async_computation.5 | async-start | bytes 21135360
  476.0 47.5 %copy-start.6 = (f32[256]{0:T(256)S(1)}, f32[256]{0:T(256)}, u32[]{:S(2)}) copy-start(f32[256]{0:T(256)} %get-tuple-element.1436) | copy-start | bytes 3076
  476.0 47.5 %copy-start.7 = (f32[256]{0:T(256)S(1)}, f32[256]{0:T(256)}, u32[]{:S(2)}) copy-start(f32[256]{0:T(256)} %get-tuple-element.1437) | copy-start | bytes 3076
  523.5 11.0 copy-start.9
  523.5 11.0 copy-start.12
  523.5 4.3 copy-start.1
  528.3 0.7 copy-start.2
  529.0 4.3 copy-start.1
  533.8 0.7 copy-start.2
  543.1 6.6 copy-start
Sparse Core Ops, SparseCore 0:
  9.7 205.7 all-gather.7
  227.5 38.6 all-gather.11
  267.9 194.0 all-gather.9
  469.8 38.6 all-gather.13
  581.9 681.1 reduce-scatter.3
where the time goes:
time: 1270 us
  waiting for transfers between devices  1110 us (87%)
  matrix products  55.1 us (4%)
  other arithmetic  45 us (4%)
  local copies, waits for them, and re-layouts  30.4 us (2%)
  blocking collectives  17.2 us (1%)
  between operations  14.1 us (1%)
    unnamed x6, waiting for transfers between devices  673 us
    all_gather x1, waiting for transfers between devices, on_device(): lax.all_gather(w_in, ('ctx', 'dp'), axis=0, tiled=True)  206 us
    all_gather x1, waiting for transfers between devices, on_device(): lax.all_gather(w_out_t, ('ctx', 'dp'), axis=0, tiled=True)  179 us
    all_gather x2, waiting for transfers between devices, entering(): lax.all_gather(part.astype(kind), axis)  50.8 us
  transfers between devices with their start and end apart: 5, of which 5 were waited for; matrix products, arithmetic and copies ran while one was open for 3% of the time, Pallas kernels for 0%

commit v1 on v0

v1 whole, which is shorter than its diff:
```python
import math

import jax
import jax.numpy as jnp
from jax import lax
from jax.experimental import pallas as pl
from jax.experimental.pallas import tpu as pltpu
from jax.sharding import PartitionSpec as P

EPSILON = 1e-06
MESH = pl.DeviceIdType.MESH
F32, BF16 = jnp.float32, jnp.bfloat16
ROWS, WIDTH, HEAD, HALF = 512, 4096, 256, 128
CENTER = ROWS // 2
Q, K, V, GATE, OUT = range(5)
EVERY = slice(None)
ORDERS = (("x", "y", "z"), ("y", "z", "x"), ("z", "x", "y"))
GATHER = [(g, h) for g in (K, V, Q, GATE, OUT) for h in (0, 1)]
REDUCE = [(g, h) for g in (OUT, GATE, Q, K, V) for h in (0, 1)]
SPLIT = {"x": "y", "y": "z", "z": "y"}
BLOCK_DIMS = {"x": (4, 4), "y": (2, 4, 2), "z": (4, 2, 2)}
PART_DIMS = {"x": (4,), "y": (4,), "z": (2, 2)}
COUNT = 4


def dot(a, b, ca, cb):
    return lax.dot_general(a, b, (((ca,), (cb,)), ((), ())), preferred_element_type=F32)


def place(half=None, x=None, y=None, z=None):
    where = {"y": EVERY if y is None else y, "z": EVERY if z is None else z}
    if half is not None:
        where[half[0]] = pl.ds(2 * half[1], 2)
    if x is None:
        return (where["y"], EVERY, where["z"], EVERY)
    return (where["y"], lax.rem(x, 2), where["z"], lax.div(x, 2))


def body(x_hbm, u_hbm, win_hbm, wout_hbm, rate_ref, gin_hbm, gwin_ref, gwout_ref,
         xv, uv, xt, ut, wg, pr, pb, sb, gp, cos_ref, sin_ref, up_ref, down_ref, qs_ref, ks_ref, v_ref, score_ref, acc_ref,
         st, gs, hid_ref, gret_ref, stage,
         tx, ty, tz, bx, by, bz, cx, cy, cz, last,
         ag_s, ag_r, st_s, st_r, gs_s, gs_r, sib_s, sib_r, rs_s, rs_r, x_sem, u_sem, w_sem, out_sem):
    ctx, dp = lax.axis_index("ctx"), lax.axis_index("dp")
    core = lax.rem(dp, 2)
    here = {
        "x": lax.rem(lax.div(dp, 2), 2) * 2 + lax.rem(ctx, 2),
        "y": lax.div(ctx, 2),
        "z": lax.div(dp, 4),
    }

    def device(at, on_core):
        return (at["y"] * 2 + lax.rem(at["x"], 2), at["z"] * 4 + lax.div(at["x"], 2) * 2 + on_core)

    def shifted(axis, by):
        return lax.rem(here[axis] + by, 4)

    def peer(axis, by):
        return device({**here, axis: shifted(axis, by)}, core)

    sibling = (ctx, dp + 1 - 2 * core)

    def remote(src, dst, send, recv, to):
        return pltpu.make_async_remote_copy(
            src_ref=src, dst_ref=dst, send_sem=send, recv_sem=recv, device_id=to, device_id_type=MESH
        )

    loads = []
    for c in range(4):
        lanes = pl.ds(c * 1024, 1024)
        for src, dst, sem in ((x_hbm, xv, x_sem), (u_hbm, uv, u_sem)):
            copy = pltpu.make_async_copy(src.at[:, lanes], dst.at[:, lanes], sem.at[c])
            loads.append(copy)
    own = []
    for n, (g, h) in enumerate(GATHER):
        rows = pl.ds(16 * h, 16)
        src = wout_hbm.at[rows] if g == OUT else win_hbm.at[rows, pl.ds(g * HEAD, HEAD)]
        copy = pltpu.make_async_copy(src, wg.at[(g,) + place(**here) + (core, h)], w_sem.at[n])
        copy.start()
        own.append(copy)
    for copy in loads:
        copy.start()

    greeted = [peer(axis, by) for axis in "xyz" for by in (1, 2, 3)] + [sibling]
    crossed = here["x"] + 1 - 2 * lax.rem(here["x"], 2)
    greeted += [device({**here, "x": crossed, "y": shifted("y", by)}, core) for by in (1, 2, 3)]
    barrier = pltpu.get_barrier_semaphore()
    for to in greeted:
        pl.semaphore_signal(barrier, inc=1, device_id=to, device_id_type=MESH)
    pl.semaphore_wait(barrier, len(greeted))

    unsent = []

    def send(src, dst, send_sem, recv_sem, to):
        copy = remote(src, dst, send_sem, recv_sem, to)
        copy.start()
        unsent.append(copy)

    def arrived(ref, recv_sem, spare):
        remote(ref, ref, spare, recv_sem, sibling).wait_recv()

    def w_at(n, **fixed):
        g, h = GATHER[n]
        return wg.at[(g,) + place(**fixed) + (core, h)]

    def ag_send(n, k, to, **fixed):
        send(w_at(n, **fixed), w_at(n, **fixed), ag_s.at[n, k], ag_r.at[n, k], to)

    def ag_wait(n, k, **fixed):
        arrived(w_at(n, **fixed), ag_r.at[n, k], ag_s.at[n, k])

    def fixed_from(order, first):
        return {a: here[a] for a in order[first:]}

    def ag_spread(n, phase):
        order = ORDERS[n % 3]
        axis, fixed = order[phase], fixed_from(order, phase)
        for k, by in enumerate((1, 3, 2)):
            ag_send(n, 3 * phase + k, peer(axis, by), **fixed)

    def ag_spread_wait(n, phase):
        order = ORDERS[n % 3]
        axis, fixed = order[phase], fixed_from(order, phase)
        for k, by in enumerate((3, 1, 2)):
            ag_wait(n, 3 * phase + k, **{**fixed, axis: shifted(axis, by)})

    def ag_last(n):
        axis = ORDERS[n % 3][2]
        ag_send(n, 6, peer(axis, 1), **{axis: here[axis]})
        ag_send(n, 7, peer(axis, 3), **{axis: here[axis]})

    def ag_relay(n):
        axis = ORDERS[n % 3][2]
        left, right = shifted(axis, 3), shifted(axis, 1)
        ag_wait(n, 6, **{axis: left})
        ag_send(n, 8, peer(axis, 1), half=(SPLIT[axis], 0), **{axis: left})
        ag_wait(n, 7, **{axis: right})
        ag_send(n, 9, peer(axis, 3), half=(SPLIT[axis], 1), **{axis: right})

    def ag_opposite(n):
        axis = ORDERS[n % 3][2]
        far = shifted(axis, 2)
        ag_wait(n, 8, half=(SPLIT[axis], 0), **{axis: far})
        ag_wait(n, 9, half=(SPLIT[axis], 1), **{axis: far})
        ag_send(n, 10, sibling)

    def ag_done(n):
        g, h = GATHER[n]
        arrived(wg.at[(g,) + place() + (1 - core, h)], ag_r.at[n, 10], ag_s.at[n, 10])

    units = range(len(GATHER))
    for copy in own:
        copy.wait()
    for n in units:
        ag_spread(n, 0)

    rate = rate_ref[...]
    row = lax.broadcasted_iota(jnp.int32, (ROWS, HALF), 0).astype(F32)
    spacing = jnp.exp(
        lax.broadcasted_iota(jnp.int32, (1, HALF), 1).astype(F32) * (-math.log(10000.0) / HALF)
    )
    angle = (row + (ctx * ROWS).astype(F32)) * spacing
    cos_ref[...] = jnp.cos(angle)
    sin_ref[...] = jnp.sin(angle)
    up_ref[...] = jnp.exp((CENTER - row) * rate)
    down_ref[...] = jnp.exp((row - CENTER) * rate)
    rates = jnp.concatenate([rate, rate], axis=1)

    for n in units:
        ag_spread_wait(n, 0)
        ag_spread(n, 1)
    waves = [units[0:4], units[4:8], units[8:10]]
    for n in units:
        ag_spread_wait(n, 1)
        if n in waves[0]:
            ag_last(n)
    for copy in loads:
        copy.wait()

    def transpose(src, dst):
        def step(c, _):
            at = pl.ds(pl.multiple_of(c * 256, 256), 256)
            dst[at, :] = src[:, at].T
            return _
        lax.fori_loop(0, WIDTH // 256, step, 0)

    transpose(xv, xt)
    for n in waves[0]:
        ag_relay(n)
    for n in waves[1]:
        ag_last(n)
    transpose(uv, ut)
    for n in waves[0]:
        ag_opposite(n)

    def project(g):
        for n, (group, _) in enumerate(GATHER):
            if group == g:
                ag_done(n)
        left = uv if g == OUT else xv
        pr[g] = dot(left[...], wg[g].reshape(WIDTH, HEAD), 1, 0)

    def rotated(a):
        a = a.astype(BF16).astype(F32)
        a1, a2 = a[:, :HALF], a[:, HALF:]
        cos, sin = cos_ref[...], sin_ref[...]
        return jnp.concatenate([a1 * cos - a2 * sin, a1 * sin + a2 * cos], axis=1).astype(BF16).astype(F32)

    def unrotated(g):
        g1, g2 = g[:, :HALF], g[:, HALF:]
        cos, sin = cos_ref[...], sin_ref[...]
        return jnp.concatenate([g1 * cos + g2 * sin, g2 * cos - g1 * sin], axis=1).astype(BF16)

    def twice(t):
        return jnp.concatenate([t, t], axis=1)

    for n in waves[1]:
        ag_relay(n)
    for n in waves[2]:
        ag_last(n)
    project(K)
    ks_ref[...] = (rotated(pr[K]) * twice(down_ref[...])).astype(BF16)
    project(V)
    v_ref[...] = pr[V].astype(BF16)
    st[ctx] = (dot(v_ref[...], ks_ref[...], 0, 0) * jnp.exp(-(CENTER - 1.0) * rates)).astype(BF16)

    def each_later(act):
        for d in range(1, 8):
            @pl.when(ctx + d < 8)
            def _():
                act(remote(st.at[ctx], st.at[ctx], st_s.at[d - 1], st_r.at[ctx], (ctx + d, dp)))

    each_later(lambda copy: copy.start())
    for n in waves[2]:
        ag_relay(n)
    for n in waves[1]:
        ag_opposite(n)
    project(Q)
    qs_ref[...] = (rotated(pr[Q]) * twice(up_ref[...])).astype(BF16)
    for n in waves[2]:
        ag_opposite(n)
    project(GATE)
    before = lax.broadcasted_iota(jnp.int32, (ROWS, ROWS), 0) >= lax.broadcasted_iota(jnp.int32, (ROWS, ROWS), 1)
    score_ref[...] = jnp.where(before, dot(qs_ref[...], ks_ref[...], 1, 1), 0.0).astype(BF16)
    project(OUT)

    shard_decay = jnp.exp(-float(ROWS) * rates)
    acc_ref[...] = jnp.zeros_like(acc_ref)

    def take(i, _):
        arrived(st.at[i], st_r.at[i], st_s.at[0])
        acc_ref[...] = acc_ref[...] * shard_decay + st[i].astype(F32)
        return _

    lax.fori_loop(0, ctx, take, 0)
    state = (acc_ref[...] * jnp.exp(-(CENTER + 1.0) * rates)).astype(BF16)

    retained = dot(score_ref[...], v_ref[...], 1, 0) + dot(qs_ref[...], state, 1, 1)
    inverse = lax.rsqrt(jnp.mean(retained * retained, axis=1, keepdims=True) + EPSILON)
    normed = retained * inverse
    gate = pr[GATE].astype(BF16).astype(F32)
    grad_hidden = pr[OUT]
    sig = jax.nn.sigmoid(gate)
    hid_ref[...] = (gate * sig * normed).astype(BF16)
    grad_normed = grad_hidden * gate * sig
    gp[:, GATE * HEAD:] = (grad_hidden * normed * sig * (1.0 + gate * (1.0 - sig))).astype(BF16)
    gret_ref[...] = (
        inverse * (grad_normed - normed * jnp.mean(grad_normed * normed, axis=1, keepdims=True))
    ).astype(BF16)

    gs[ctx] = (dot(gret_ref[...], qs_ref[...], 0, 0) * jnp.exp(-float(CENTER) * rates)).astype(BF16)

    def each_earlier(act):
        for d in range(1, 8):
            @pl.when(ctx - d >= 0)
            def _():
                act(remote(gs.at[ctx], gs.at[ctx], gs_s.at[d - 1], gs_r.at[ctx], (ctx - d, dp)))

    each_earlier(lambda copy: copy.start())

    def term(g):
        left = ut if g == OUT else xt

        def step(c, _):
            right = hid_ref[...] if g == OUT else gp[:, g * HEAD:(g + 1) * HEAD]
            rows = pl.ds(pl.multiple_of(c * 1024, 1024), 1024)
            pb[g, c] = dot(left[rows, :], right, 1, 0).astype(BF16).reshape(2, 4, 2, 2, 2, 16, HEAD)
            return _

        lax.fori_loop(0, 4, step, 0)
        send(pb.at[(g,) + place() + (1 - core,)], sb.at[g], sib_s.at[g], sib_r.at[g], sibling)

    def pair(g):
        arrived(sb.at[g], sib_r.at[g], sib_s.at[g])

        def step(c, _):
            mine = pb[g, c, :, :, :, core]
            sb[g, c] = (sb[g, c].astype(F32) + mine.astype(F32)).astype(BF16)
            return _

        lax.fori_loop(0, 4, step, 0)

    opposite = {"x": tx, "y": ty, "z": tz}
    blocks = {"x": bx, "y": by, "z": bz}
    parts = {"x": cx, "y": cy, "z": cz}

    def s_idx(n, **fixed):
        g, h = REDUCE[n]
        return (g,) + place(**fixed) + (h,)

    def t_at(n, side):
        axis = ORDERS[n % 3][2]
        half = pl.ds(2 * side, 2)
        return opposite[axis].at[(n // 3, EVERY, half) if axis == "y" else (n // 3, half)]

    def rs_first(n):
        axis = ORDERS[n % 3][2]
        far = shifted(axis, 2)
        for side, by in ((0, 1), (1, 3)):
            src = sb.at[s_idx(n, half=(SPLIT[axis], side), **{axis: far})]
            send(src, t_at(n, side), rs_s.at[n, side], rs_r.at[n, side], peer(axis, by))

    def rs_second(n):
        axis = ORDERS[n % 3][2]
        for side, by in ((0, 1), (1, 3)):
            arrived(t_at(n, side), rs_r.at[n, side], rs_s.at[n, side])
            at = s_idx(n, half=(SPLIT[axis], side), **{axis: shifted(axis, by)})
            sb[at] = (sb[at].astype(F32) + t_at(n, side)[...].astype(F32)).astype(BF16)
            send(sb.at[s_idx(n, **{axis: shifted(axis, by)})], blocks[axis].at[n // 3, side],
                 rs_s.at[n, 2 + side], rs_r.at[n, 2 + side], peer(axis, by))

    def rs_third(n):
        a1, a2, a3 = ORDERS[n % 3]
        for side in (0, 1):
            ref = blocks[a3].at[n // 3, side]
            arrived(ref, rs_r.at[n, 2 + side], rs_s.at[n, 2 + side])
        at = s_idx(n, **{a3: here[a3]})
        got = blocks[a3]
        sb[at] = (sb[at].astype(F32) + got[n // 3, 0].astype(F32) + got[n // 3, 1].astype(F32)).astype(BF16)
        for k, by in enumerate((1, 3, 2)):
            src = sb.at[s_idx(n, **{a3: here[a3], a2: shifted(a2, by)})]
            send(src, parts[a3].at[n // 3, k], rs_s.at[n, 4 + k], rs_r.at[n, 4 + k], peer(a2, by))

    def rs_fourth(n):
        a1, a2, a3 = ORDERS[n % 3]
        got = parts[a3]
        for k in range(3):
            arrived(got.at[n // 3, k], rs_r.at[n, 4 + k], rs_s.at[n, 4 + k])
        at = s_idx(n, **{a3: here[a3], a2: here[a2]})
        total = sb[at].astype(F32)
        for k in range(3):
            total += got[n // 3, k].astype(F32)
        sb[at] = total.astype(BF16)
        for k, by in enumerate((1, 3, 2)):
            src = sb.at[s_idx(n, **{a3: here[a3], a2: here[a2], a1: shifted(a1, by)})]
            send(src, last.at[n, k], rs_s.at[n, 7 + k], rs_r.at[n, 7 + k], peer(a1, by))

    def rs_end(n):
        g, h = REDUCE[n]
        for k in range(3):
            arrived(last.at[n, k], rs_r.at[n, 7 + k], rs_s.at[n, 7 + k])
        total = sb[s_idx(n, **here)].astype(F32)
        for k in range(3):
            total += last[n, k].astype(F32)
        if g == OUT:
            gwout_ref[16 * h:16 * h + 16, :] = total
        else:
            gwin_ref[16 * h:16 * h + 16, g * HEAD:(g + 1) * HEAD] = total

    puts = []

    def grad_input(c):
        slot = c % 2
        if c >= 2:
            puts[c - 2].wait()
        w = jnp.concatenate([wg[g, c].reshape(1024, HEAD) for g in (Q, K, V, GATE)], axis=1)
        stage[slot] = dot(gp[...], w, 1, 1).astype(BF16)
        put = pltpu.make_async_copy(stage.at[slot], gin_hbm.at[:, pl.ds(c * 1024, 1024)], out_sem.at[c])
        put.start()
        puts.append(put)

    term(OUT)
    term(GATE)
    score_grad = jnp.where(before, dot(gret_ref[...], v_ref[...], 1, 1), 0.0).astype(BF16)
    pr[Q] = dot(score_grad, ks_ref[...], 1, 0) + dot(gret_ref[...], state, 1, 0)
    pair(OUT)
    for n in (0, 1):
        rs_first(n)
    pr[K] = dot(score_grad, qs_ref[...], 0, 0)
    pair(GATE)
    for n in (2, 3):
        rs_first(n)
    gp[:, Q * HEAD:(Q + 1) * HEAD] = unrotated(pr[Q] * twice(up_ref[...]))
    term(Q)
    pr[V] = dot(score_ref[...], gret_ref[...], 0, 0)
    for n in (0, 1):
        rs_second(n)
    acc_ref[...] = jnp.zeros_like(acc_ref)

    def take_back(j, _):
        i = 7 - j
        arrived(gs.at[i], gs_r.at[i], gs_s.at[0])
        acc_ref[...] = acc_ref[...] * shard_decay + gs[i].astype(F32)
        return _

    lax.fori_loop(0, 7 - ctx, take_back, 0)
    grad_state = (acc_ref[...] * jnp.exp(-float(CENTER) * rates)).astype(BF16)
    gp[:, K * HEAD:(K + 1) * HEAD] = unrotated(
        (pr[K] + dot(v_ref[...], grad_state, 1, 0)) * twice(down_ref[...])
    )
    term(K)
    pair(Q)
    for n in (4, 5):
        rs_first(n)
    for n in (2, 3):
        rs_second(n)
    gp[:, V * HEAD:(V + 1) * HEAD] = (pr[V] + dot(ks_ref[...], grad_state, 1, 1)).astype(BF16)
    term(V)
    pair(K)
    for n in (6, 7):
        rs_first(n)
    pair(V)
    for n in (8, 9):
        rs_first(n)
    for n in (0, 1):
        rs_third(n)
    for n in (4, 5):
        rs_second(n)
    grad_input(0)
    for n in (2, 3):
        rs_third(n)
    for n in (6, 7):
        rs_second(n)
    for n in (8, 9):
        rs_second(n)
    grad_input(1)
    for n in (0, 1, 2, 3):
        rs_fourth(n)
    for n in (4, 5):
        rs_third(n)
    grad_input(2)
    for n in (6, 7, 8, 9):
        rs_third(n)
    grad_input(3)
    for n in (4, 5, 6, 7, 8, 9):
        rs_fourth(n)
    for n in range(10):
        rs_end(n)
    for put in puts[2:]:
        put.wait()
    for copy in unsent:
        copy.wait_send()
    each_later(lambda copy: copy.wait_send())
    each_earlier(lambda copy: copy.wait_send())


def on_device(layer_input, grad_out, w_in, w_out_t, decay_rate):
    hbm, vmem = pl.BlockSpec(memory_space=pl.ANY), pl.BlockSpec(memory_space=pltpu.VMEM)
    dma = pltpu.SemaphoreType.DMA
    buf = pltpu.VMEM
    grad_in, grad_w, grad_wo = pl.pallas_call(
        body,
        out_shape=(
            jax.ShapeDtypeStruct((ROWS, WIDTH), BF16),
            jax.ShapeDtypeStruct((32, 4 * HEAD), F32),
            jax.ShapeDtypeStruct((32, HEAD), F32),
        ),
        in_specs=[hbm, hbm, hbm, hbm, vmem],
        out_specs=(hbm, vmem, vmem),
        scratch_shapes=[
            buf((ROWS, WIDTH), BF16),
            buf((ROWS, WIDTH), BF16),
            buf((WIDTH, ROWS), BF16),
            buf((WIDTH, ROWS), BF16),
            buf((5, 4, 2, 4, 2, 2, 2, 16, HEAD), BF16),
            buf((5, ROWS, HEAD), F32),
            buf((5, 4, 2, 4, 2, 2, 2, 16, HEAD), BF16),
            buf((5, 4, 2, 4, 2, 2, 16, HEAD), BF16),
            buf((ROWS, 4 * HEAD), BF16),
            buf((ROWS, HALF), F32), buf((ROWS, HALF), F32), buf((ROWS, HALF), F32), buf((ROWS, HALF), F32),
            buf((ROWS, HEAD), BF16), buf((ROWS, HEAD), BF16), buf((ROWS, HEAD), BF16),
            buf((ROWS, ROWS), BF16),
            buf((HEAD, HEAD), F32),
            buf((8, HEAD, HEAD), BF16), buf((8, HEAD, HEAD), BF16),
            buf((ROWS, HEAD), BF16), buf((ROWS, HEAD), BF16),
            buf((2, ROWS, 1024), BF16),
            *[buf((COUNT,) + BLOCK_DIMS[a] + (16, HEAD), BF16) for a in "xyz"],
            *[buf((COUNT, 2) + BLOCK_DIMS[a] + (16, HEAD), BF16) for a in "xyz"],
            *[buf((COUNT, 3) + PART_DIMS[a] + (16, HEAD), BF16) for a in "xyz"],
            buf((10, 3, 16, HEAD), BF16),
            dma((10, 11)), dma((10, 11)),
            dma((7,)), dma((8,)), dma((7,)), dma((8,)),
            dma((5,)), dma((5,)),
            dma((10, 10)), dma((10, 10)),
            dma((4,)), dma((4,)), dma((10,)), dma((4,)),
        ],
        compiler_params=pltpu.CompilerParams(
            collective_id=0, has_side_effects=True, vmem_limit_bytes=62 * 1024 * 1024
        ),
        cost_estimate=pl.CostEstimate(flops=17 * 10**9, bytes_accessed=13 * 10**6, transcendentals=10**6),
        name="retention_backward",
    )(layer_input[0], grad_out[0], w_in, w_out_t, decay_rate[None, :])
    return grad_in[None], grad_w, grad_wo


def solution(mesh):
    rows = P(("ctx", "dp"), None)
    tokens = P("dp", "ctx", None)
    return jax.shard_map(
        on_device,
        mesh=mesh,
        in_specs=(tokens, tokens, rows, rows, P()),
        out_specs=(tokens, rows, rows),
        check_vma=False,
    )
```

time: 1270 us -> 111 us (0.09)
  waiting for transfers between devices: 1110 us -> 0 us
  Pallas kernels: 0 us -> 104 us
  matrix products: 55.1 us -> 0 us
  other arithmetic: 45 us -> 0 us
  local copies, waits for them, and re-layouts: 30.4 us -> 6.01 us
  blocking collectives: 17.2 us -> 0 us
  between operations: 14.1 us -> 0.66 us
    unnamed x6 -> x0, waiting for transfers between devices: 673 us -> none
    all_gather x4 -> x0, waiting for transfers between devices: 436 us -> none  [the longest x1 206 us: on_device(): lax.all_gather(w_in, ('ctx', 'dp'), axis=0, tiled=True)]
    pallas_call x0 -> x1, Pallas kernels: none -> 104 us  [on_device(): pl.pallas_call(body, out_shape=(jax.ShapeDtypeStruct((ROWS, WIDTH), BF16)...]
    dot_general x33 -> x0, matrix products: 55.1 us -> none  [the longest x1 9.47 us: on_device(): lax.dot_general(grad_proj, w_in_all, (((1,), (1,)), ((), ())), preferred_...]
    unnamed x31 -> x7, local copies, waits for them, and re-layouts: 24.8 us -> 6.01 us
    all_gather x1 -> x0, blocking collectives: 17.2 us -> none  [entering(): lax.all_gather(part.astype(kind), axis)]
    select_n x16 -> x0, other arithmetic: 16.5 us -> none  [step(): return jax.tree.map(lambda a, b: jnp.where(reached, a, b), new, before)]
  transfers between devices with their start and end apart: 5 -> 0, of which waited for: 5 -> 0; matrix products, arithmetic and copies ran while one was open for 3% -> 0% of each run, Pallas kernels for 0% -> 0%
where the time goes in v1:
time: 111 us
  Pallas kernels  104 us (94%)
  local copies, waits for them, and re-layouts  6.01 us (5%)
    pallas_call x1, Pallas kernels, on_device(): pl.pallas_call(body, out_shape=(jax.ShapeDtypeStruct((ROWS, WIDTH), BF16)...  104 us
    unnamed x7, local copies, waits for them, and re-layouts  6.01 us

profile of v1, /device:TPU:0, one launch (start us, length us, event | category | flops | bytes accessed | tf_op | source)
XLA Modules:
  0.0 110.7 jit_solution(9900538203136057441)
XLA Ops:
  0.6 104.1 %retention_backward.1 = (bf16[512,4096]{1,0:T(8,128)(2,1)}, f32[32,1024]{1,0:T(8,128)}, f32[32,256]{1,0:T(8,128)}) custom-call(bf16[512,4096]{1,0:T(8,128)(2,1)} %bitcast.5, bf16[512,4096]{1,0:T(8,128)(2,1)} %bitcast.6, bf16[32,1024]{1,0:T(8,128)(2,1)} %win_hbm.1, bf16[32,256]{1,0:T(8,128)(2,1)} %wout_hbm.1, f32[1,128]{1,0:T(1,128)} %bitcast.7), custom_call_target="tpu_custom_call" | custom-call | flops 16999999488 | bytes 13000000 | tf_op jit(solution)/shard_map/retention_backward/pallas_call | solution.py:461
  104.7 0.0 copy-start
  104.7 0.0 copy-start.1
  104.7 4.7 %copy.11 = bf16[1,512,4096]{2,1,0:T(8,128)(2,1)} copy(bf16[1,512,4096]{2,1,0:T(8,128)(2,1)} %bitcast.4) | data formatting | bytes 8388608
  109.5 0.0 copy-done
  109.5 0.7 copy.12
  110.1 0.0 copy-done.1
  110.1 0.6 copy.13
Async XLA Ops:
  104.7 4.8 %copy-start = (f32[32,1024]{1,0:T(8,128)S(1)}, f32[32,1024]{1,0:T(8,128)}, u32[]{:S(2)}) copy-start(f32[32,1024]{1,0:T(8,128)} %get-tuple-element.13) | copy-start | bytes 393220
  104.7 5.4 %copy-start.1 = (f32[32,256]{1,0:T(8,128)S(1)}, f32[32,256]{1,0:T(8,128)}, u32[]{:S(2)}) copy-start(f32[32,256]{1,0:T(8,128)} %get-tuple-element.14) | copy-start | bytes 98308

commit v2 on v1

v2 whole, which is shorter than its diff:
```python
import math

import jax
import jax.numpy as jnp
from jax import lax
from jax.experimental import pallas as pl
from jax.experimental.pallas import tpu as pltpu
from jax.sharding import PartitionSpec as P

EPSILON = 1e-06
MESH = pl.DeviceIdType.MESH
F32, BF16 = jnp.float32, jnp.bfloat16
ROWS, WIDTH, HEAD, HALF = 512, 4096, 256, 128
CENTER = ROWS // 2
K, V, Q, GATE, OUT = range(5)
EVERY = slice(None)
ORDERS = (("x", "y", "z"), ("y", "z", "x"), ("z", "x", "y"))
PIECES = (
    (0, slice(0, 384), 256), (1, slice(0, 384), 256), (EVERY, slice(384, 512), 640),
    (EVERY, slice(512, 768), 0), (EVERY, slice(768, 1024), 768), (EVERY, slice(1024, 1280), None),
)
KV, QGO = (0, 1, 2), (3, 4, 5)
SPLIT = {"x": "y", "y": "z", "z": "y"}
BLOCK_DIMS = {"x": (4, 4), "y": (2, 4, 2), "z": (4, 2, 2)}
PART_DIMS = {"x": (4,), "y": (4,), "z": (2, 2)}


def inner(n):
    rows, lanes, _ = PIECES[n]
    return ((2,) if rows == EVERY else ()) + (16, lanes.stop - lanes.start)


def lanes_of(g):
    return slice(g * HEAD, (g + 1) * HEAD)


def dot(a, b, ca, cb):
    return lax.dot_general(a, b, (((ca,), (cb,)), ((), ())), preferred_element_type=F32)


def place(half=None, x=None, y=None, z=None):
    where = {"y": EVERY if y is None else y, "z": EVERY if z is None else z}
    if half is not None and half[0] != "x":
        where[half[0]] = pl.ds(2 * half[1], 2)
    if x is None:
        return (where["y"], EVERY, where["z"], pl.ds(half[1], 1) if half is not None and half[0] == "x" else EVERY)
    return (where["y"], lax.rem(x, 2), where["z"], lax.div(x, 2))


def body(x_hbm, u_hbm, win_hbm, wout_hbm, rate_ref, gin_hbm, gwin_ref, gwout_ref,
         xv, uv, xt, ut, wg, pr, pb, sb, gp, cos_ref, sin_ref, up_ref, down_ref, qs_ref, ks_ref, v_ref, score_ref, acc_ref,
         st, st_pair, st_y, st_sum, gs, gs_pair, gs_y, gs_sum, hid_ref, gret_ref, stage, *rest):
    far_a, near_a, far_b, near_b, last = (rest[6 * k:6 * k + 6] for k in range(5))
    ag_s, ag_r, st_s, st_r, gs_s, gs_r, sib_s, sib_r, rs_s, rs_r, load_sem, out_sem = rest[30:]
    ctx, dp = lax.axis_index("ctx"), lax.axis_index("dp")
    core = lax.rem(dp, 2)
    here = {
        "x": lax.rem(lax.div(dp, 2), 2) * 2 + lax.rem(ctx, 2),
        "y": lax.div(ctx, 2),
        "z": lax.div(dp, 4),
    }

    def device(at, on_core):
        return (at["y"] * 2 + lax.rem(at["x"], 2), at["z"] * 4 + lax.div(at["x"], 2) * 2 + on_core)

    def shifted(axis, by):
        return lax.rem(here[axis] + by, 4)

    def peer(axis, by):
        return device({**here, axis: shifted(axis, by)}, core)

    sibling = (ctx, dp + 1 - 2 * core)

    def remote(src, dst, send, recv, to):
        return pltpu.make_async_remote_copy(
            src_ref=src, dst_ref=dst, send_sem=send, recv_sem=recv, device_id=to, device_id_type=MESH
        )

    mine = place(**here) + (core,)
    own = wg.at[mine]
    for src, first, to, size in ((win_hbm, HEAD, K, 2), (win_hbm, 0, Q, 1), (win_hbm, 3 * HEAD, GATE, 1), (wout_hbm, 0, OUT, 1)):
        src = src.at[:, :, pl.ds(first, size * HEAD)]
        pltpu.make_async_copy(src, wg.at[mine + (EVERY, EVERY, pl.ds(to * HEAD, size * HEAD))], load_sem.at[2]).start()
    load_x = pltpu.make_async_copy(x_hbm, xv, load_sem.at[0])
    load_u = pltpu.make_async_copy(u_hbm, uv, load_sem.at[1])
    load_x.start()
    load_u.start()

    greeted = [peer(axis, by) for axis in "xyz" for by in (1, 2, 3)] + [sibling]
    barrier = pltpu.get_barrier_semaphore()
    for to in greeted:
        pl.semaphore_signal(barrier, inc=1, device_id=to, device_id_type=MESH)
    pl.semaphore_wait(barrier, len(greeted))

    def send(src, dst, send_sem, recv_sem, to):
        remote(src, dst, send_sem, recv_sem, to).start()

    def arrived(ref, recv_sem):
        remote(ref, ref, ag_s.at[0], recv_sem, sibling).wait_recv()

    def sent(ref, send_sem):
        remote(ref, ref, send_sem, ag_r.at[0, 0], sibling).wait_send()

    def w_at(n, **fixed):
        rows, lanes, _ = PIECES[n]
        return wg.at[place(**fixed) + (core, rows, EVERY, lanes)]

    W_BYTES = ((slice(0, 3), 0, 0, 0), (slice(0, 2), 0, EVERY, 0), (slice(0, 1), 0, EVERY, 0),
               (slice(0, 2), EVERY, EVERY, EVERY), (0, EVERY, EVERY, EVERY), (EVERY, EVERY, EVERY, EVERY))

    def ag_send(n, step, to, **fixed):
        send(w_at(n, **fixed), w_at(n, **fixed), ag_s.at[step], ag_r.at[n, step], to)

    def ag_wait(n, step):
        rows, lanes, _ = PIECES[n]
        arrived(wg.at[W_BYTES[step] + (0, rows, EVERY, lanes)], ag_r.at[n, step])

    def ag_first(n):
        axis = ORDERS[n % 3][0]
        for by in (1, 3, 2):
            ag_send(n, 0, peer(axis, by), **here)

    def ag_both(n, k):
        order = ORDERS[n % 3]
        axis, fixed = order[k], {a: here[a] for a in order[k:]}
        for by in (1, 3):
            ag_send(n, 2 * k - 1, peer(axis, by), **fixed)
        if k == 2:
            ag_send(n, 5, sibling, **fixed)

    def ag_relay(n, k):
        order = ORDERS[n % 3]
        axis, fixed = order[k], {a: here[a] for a in order[k:]}
        split = order[0] if k == 1 else SPLIT[axis]
        ag_wait(n, 2 * k - 1)
        for by, side in ((1, 0), (3, 1)):
            ag_send(n, 2 * k, peer(axis, by), half=(split, side), **{**fixed, axis: shifted(axis, 4 - by)})
        if k == 2:
            for by in (1, 3):
                ag_send(n, 5, sibling, **{**fixed, axis: shifted(axis, by)})

    def ag_opposite(n):
        axis = ORDERS[n % 3][2]
        ag_wait(n, 4)
        ag_send(n, 5, sibling, **{axis: shifted(axis, 2)})

    def ag_done(n):
        ag_wait(n, 5)

    pltpu.make_async_copy(own, own, load_sem.at[2]).wait()
    for n in KV + QGO:
        ag_first(n)

    rate = rate_ref[...]
    row = lax.broadcasted_iota(jnp.int32, (ROWS, HALF), 0).astype(F32)
    spacing = jnp.exp(
        lax.broadcasted_iota(jnp.int32, (1, HALF), 1).astype(F32) * (-math.log(10000.0) / HALF)
    )

    def make_tables():
        angle = (row + (ctx * ROWS).astype(F32)) * spacing
        cos_ref[...] = jnp.cos(angle)
        sin_ref[...] = jnp.sin(angle)
        up_ref[...] = jnp.exp((CENTER - row) * rate)
        down_ref[...] = jnp.exp((row - CENTER) * rate)

    rates = jnp.concatenate([rate, rate], axis=1)

    def transpose(src, dst):
        def step(c, _):
            at = pl.ds(pl.multiple_of(c * 512, 512), 512)
            dst[lax.div(c, 2), lax.rem(c, 2)] = src[:, at].T.reshape(4, 2, 2, 32, ROWS)
            return _
        lax.fori_loop(0, 8, step, 0)

    make_tables()
    for n in KV + QGO:
        ag_wait(n, 0)
        ag_both(n, 1)
    for n in KV + QGO:
        ag_relay(n, 1)
    for n in KV:
        ag_wait(n, 2)
        ag_both(n, 2)
    load_x.wait()
    transpose(xv, xt)
    for n in KV:
        ag_relay(n, 2)
    for n in QGO:
        ag_wait(n, 2)
        ag_both(n, 2)
    load_u.wait()
    transpose(uv, ut)
    for n in KV:
        ag_opposite(n)

    def project(g):
        left = uv if g == OUT else xv
        pr[g] = dot(left[...], wg[..., lanes_of(g)].reshape(WIDTH, HEAD), 1, 0)

    def rotated(a):
        a = a.astype(BF16).astype(F32)
        a1, a2 = a[:, :HALF], a[:, HALF:]
        cos, sin = cos_ref[...], sin_ref[...]
        return jnp.concatenate([a1 * cos - a2 * sin, a1 * sin + a2 * cos], axis=1).astype(BF16).astype(F32)

    def unrotated(g):
        g1, g2 = g[:, :HALF], g[:, HALF:]
        cos, sin = cos_ref[...], sin_ref[...]
        return jnp.concatenate([g1 * cos + g2 * sin, g2 * cos - g1 * sin], axis=1).astype(BF16)

    def twice(t):
        return jnp.concatenate([t, t], axis=1)

    x_low = lax.rem(ctx, 2)
    pair_at = (ctx + 1 - 2 * x_low, dp)
    my_half, pair_half = pl.ds(128 * x_low, 128), pl.ds(128 * (1 - x_low), 128)
    shard_decay = jnp.exp(-float(ROWS) * rates)
    pair_decay = jnp.exp(-2.0 * ROWS * rates)

    class Exchange:
        def __init__(self, own, other, along_y, total, send_sem, recv_sem, backward):
            self.own, self.other, self.along_y, self.total = own, other, along_y, total
            self.s, self.r = send_sem, recv_sem
            self.hears, self.tells = (x_low == 0, x_low == 1) if backward else (x_low == 1, x_low == 0)
            self.backward = backward
            self.to_pair = remote(own.at[pair_half], other.at[pair_half], self.s.at[0], self.r.at[0], pair_at)
            self.to_pair_rest = remote(own.at[my_half], other.at[my_half], self.s.at[1], self.r.at[1], pair_at)
            self.halves = remote(total.at[my_half], total.at[my_half], self.s.at[2], self.r.at[2], pair_at)

        def each_y(self, act):
            for d in range(1, 4):
                to = here["y"] - d if self.backward else here["y"] + d

                @pl.when(to >= 0 if self.backward else to < 4)
                def _():
                    act(remote(self.along_y.at[here["y"]], self.along_y.at[here["y"]], self.s.at[2 + d],
                               self.r.at[3 + here["y"]], (to * 2 + x_low, dp)))

        def first(self):
            self.to_pair.start()
            pl.when(self.tells)(self.to_pair_rest.start)

        def second(self):
            self.to_pair.wait_recv()
            mine, theirs = self.own[my_half, :].astype(F32), self.other[my_half, :].astype(F32)
            near, away = jnp.where(self.tells, theirs, mine), jnp.where(self.tells, mine, theirs)
            self.along_y[here["y"]] = (shard_decay * away + near).astype(BF16)
            self.each_y(lambda copy: copy.start())

        def third(self):
            acc_ref[...] = jnp.zeros_like(acc_ref)

            def take(k, _):
                i = 3 - k if self.backward else k
                arrived(self.along_y.at[i], self.r.at[3 + i])
                acc_ref[...] = acc_ref[...] * pair_decay + self.along_y[i].astype(F32)
                return _

            lax.fori_loop(0, 3 - here["y"] if self.backward else here["y"], take, 0)
            self.total[my_half, :] = acc_ref[...].astype(BF16)
            self.halves.start()

        def result(self):
            self.halves.wait_recv()
            pl.when(self.hears)(self.to_pair_rest.wait_recv)
            total = self.total[...].astype(F32)
            return jnp.where(self.hears, shard_decay * total + self.other[...].astype(F32), total)

        def sent(self):
            self.to_pair.wait_send()
            pl.when(self.tells)(self.to_pair_rest.wait_send)
            self.each_y(lambda copy: copy.wait_send())
            self.halves.wait_send()

    states = Exchange(st, st_pair, st_y, st_sum, st_s, st_r, False)
    grad_states = Exchange(gs, gs_pair, gs_y, gs_sum, gs_s, gs_r, True)

    ag_done(0)
    ag_done(1)
    project(K)
    ks_ref[...] = (rotated(pr[K]) * twice(down_ref[...])).astype(BF16)
    ag_done(2)
    project(V)
    v_ref[...] = pr[V].astype(BF16)
    st[...] = (dot(v_ref[...], ks_ref[...], 0, 0) * jnp.exp(-(CENTER - 1.0) * rates)).astype(BF16)
    states.first()
    for n in QGO:
        ag_relay(n, 2)
    states.second()
    for n in QGO:
        ag_opposite(n)
    states.third()
    ag_done(3)
    project(Q)
    qs_ref[...] = (rotated(pr[Q]) * twice(up_ref[...])).astype(BF16)
    before = lax.broadcasted_iota(jnp.int32, (ROWS, ROWS), 0) >= lax.broadcasted_iota(jnp.int32, (ROWS, ROWS), 1)
    score_ref[...] = jnp.where(before, dot(qs_ref[...], ks_ref[...], 1, 1), 0.0).astype(BF16)
    ag_done(4)
    project(GATE)
    state = (states.result() * jnp.exp(-(CENTER + 1.0) * rates)).astype(BF16)
    retained = dot(score_ref[...], v_ref[...], 1, 0) + dot(qs_ref[...], state, 1, 1)
    inverse = lax.rsqrt(jnp.mean(retained * retained, axis=1, keepdims=True) + EPSILON)
    normed = retained * inverse

    ag_done(5)
    project(OUT)
    gate = pr[GATE].astype(BF16).astype(F32)
    grad_hidden = pr[OUT]
    sig = jax.nn.sigmoid(gate)
    hid_ref[...] = (gate * sig * normed).astype(BF16)
    grad_normed = grad_hidden * gate * sig
    gp[:, lanes_of(GATE)] = (grad_hidden * normed * sig * (1.0 + gate * (1.0 - sig))).astype(BF16)
    gret_ref[...] = (
        inverse * (grad_normed - normed * jnp.mean(grad_normed * normed, axis=1, keepdims=True))
    ).astype(BF16)

    gs[...] = (dot(gret_ref[...], qs_ref[...], 0, 0) * jnp.exp(-float(CENTER) * rates)).astype(BF16)
    grad_states.first()

    def half_term(g, c, of_core):
        left = ut if g == OUT else xt
        right = hid_ref[...] if g == OUT else gp[:, lanes_of(g)]
        return dot(left[pl.ds(2 * c, 2), :, :, :, of_core].reshape(1024, ROWS), right, 1, 0).reshape(2, 2, 4, 2, 2, 16, HEAD)

    def term(g):
        def step(c, _):
            pb[pl.ds(2 * c, 2), ..., lanes_of(g)] = half_term(g, c, 1 - core).astype(BF16)
            return _

        lax.fori_loop(0, 2, step, 0)
        lanes = pl.ds(g * HEAD, HEAD)
        at = (EVERY,) * 6 + (lanes,)
        send(pb.at[at], sb.at[at], sib_s.at[0], sib_r.at[g], sibling)

    def pair(g):
        arrived(sb.at[(EVERY,) * 6 + (pl.ds(g * HEAD, HEAD),)], sib_r.at[g])

        def step(c, _):
            at = (pl.ds(2 * c, 2),) + (EVERY,) * 5 + (lanes_of(g),)
            sb[at] = (half_term(g, c, core) + sb[at].astype(F32)).astype(BF16)
            return _

        lax.fori_loop(0, 2, step, 0)

    def s_idx(n, **fixed):
        rows, lanes, _ = PIECES[n]
        return place(**fixed) + (rows, EVERY, lanes)

    def rs_axis(n, k):
        a1, a2, a3 = ORDERS[n % 3]
        if k == 0:
            return a3, SPLIT[a3], {}, far_a[n], near_a[n]
        return a2, a1, {a3: here[a3]}, far_b[n], near_b[n]

    def half_of(n, k, side):
        axis, split, _, far, _ = rs_axis(n, k)
        half = pl.ds(side, 1) if split == "x" else pl.ds(2 * side, 2)
        return far.at[(EVERY, half) if split == "x" or (k == 0 and axis == "y") else (half,)]

    def rs_first(n, k):
        axis, split, fixed, _, _ = rs_axis(n, k)
        far = shifted(axis, 2)
        for side, by in ((0, 1), (1, 3)):
            src = sb.at[s_idx(n, half=(split, side), **{**fixed, axis: far})]
            send(src, half_of(n, k, side), rs_s.at[2 * k], rs_r.at[n, 2 * k], peer(axis, by))

    def rs_second(n, k):
        axis, split, fixed, far, near = rs_axis(n, k)
        arrived(far, rs_r.at[n, 2 * k])
        for side, by in ((0, 1), (1, 3)):
            at = s_idx(n, half=(split, side), **{**fixed, axis: shifted(axis, by)})
            sb[at] = (sb[at].astype(F32) + half_of(n, k, side)[...].astype(F32)).astype(BF16)
            send(sb.at[s_idx(n, **{**fixed, axis: shifted(axis, by)})], near.at[side],
                 rs_s.at[2 * k + 1], rs_r.at[n, 2 * k + 1], peer(axis, by))

    def rs_third(n, k):
        axis, _, fixed, _, near = rs_axis(n, k)
        arrived(near, rs_r.at[n, 2 * k + 1])
        at = s_idx(n, **{**fixed, axis: here[axis]})
        sb[at] = (sb[at].astype(F32) + near[0].astype(F32) + near[1].astype(F32)).astype(BF16)
        if k == 0:
            rs_first(n, 1)
            return
        a1 = ORDERS[n % 3][0]
        for k, by in enumerate((1, 3, 2)):
            src = sb.at[s_idx(n, **{**here, a1: shifted(a1, by)})]
            send(src, last[n].at[k], rs_s.at[4], rs_r.at[n, 4], peer(a1, by))

    def rs_end(n):
        rows, lanes, to = PIECES[n]
        arrived(last[n], rs_r.at[n, 4])
        total = sb[s_idx(n, **here)].astype(F32)
        for k in range(3):
            total += last[n][k].astype(F32)
        total = total.reshape(-1, total.shape[-1])
        out_rows = EVERY if rows == EVERY else slice(16 * rows, 16 * rows + 16)
        if to is None:
            gwout_ref[out_rows, :] = total
        else:
            gwin_ref[out_rows, slice(to, to + total.shape[-1])] = total

    puts = []

    def grad_input(c):
        slot = c % 2
        if c >= 2:
            puts[c - 2].wait()
        stage[slot] = dot(gp[...], wg[c, ..., slice(0, 4 * HEAD)].reshape(1024, 4 * HEAD), 1, 1).astype(BF16)
        put = pltpu.make_async_copy(stage.at[slot], gin_hbm.at[:, pl.ds(c * 1024, 1024)], out_sem.at[slot])
        put.start()
        puts.append(put)

    term(OUT)
    term(GATE)
    grad_states.second()
    score_grad = jnp.where(before, dot(gret_ref[...], v_ref[...], 1, 1), 0.0).astype(BF16)
    grad_q = dot(score_grad, ks_ref[...], 1, 0) + dot(gret_ref[...], state, 1, 0)
    gp[:, lanes_of(Q)] = unrotated(grad_q * twice(up_ref[...]))
    term(Q)
    pair(OUT)
    rs_first(5, 0)
    pair(GATE)
    rs_first(4, 0)
    grad_states.third()
    pair(Q)
    rs_first(3, 0)
    grad_k = dot(score_grad, qs_ref[...], 0, 0)
    rs_second(5, 0)
    rs_second(4, 0)
    grad_state = (grad_states.result() * jnp.exp(-float(CENTER) * rates)).astype(BF16)
    gp[:, lanes_of(K)] = unrotated((grad_k + dot(v_ref[...], grad_state, 1, 0)) * twice(down_ref[...]))
    term(K)
    rs_second(3, 0)
    grad_v = dot(score_ref[...], gret_ref[...], 0, 0) + dot(ks_ref[...], grad_state, 1, 1)
    gp[:, lanes_of(V)] = grad_v.astype(BF16)
    term(V)
    pair(K)
    pair(V)
    for n in KV:
        rs_first(n, 0)
    grad_input(0)
    for n in (5, 4, 3):
        rs_third(n, 0)
    grad_input(1)
    for n in KV:
        rs_second(n, 0)
    for n in (5, 4, 3):
        rs_second(n, 1)
    grad_input(2)
    for n in (5, 4, 3):
        rs_third(n, 1)
    for n in KV:
        rs_third(n, 0)
    grad_input(3)
    for n in KV:
        rs_second(n, 1)
    for n in (5, 4, 3):
        rs_end(n)
    for n in KV:
        rs_third(n, 1)
    for n in KV:
        rs_end(n)
    for put in puts[2:]:
        put.wait()
    for step, of in enumerate(W_BYTES):
        sent(wg.at[of + (0,)], ag_s.at[step])
    sent(sb, sib_s.at[0])
    for step, of in enumerate(((0,), (slice(0, 2),), (slice(0, 1), 0, EVERY, 0), (slice(0, 2), 0, EVERY, 0), (slice(0, 3), 0, 0, 0))):
        sent(sb.at[of], rs_s.at[step])
    states.sent()
    grad_states.sent()


def publish(a, b, c, a_out, b_out, c_out, sem):
    copies = [pltpu.make_async_copy(b, b_out, sem.at[0]), pltpu.make_async_copy(c, c_out, sem.at[1])]
    for k in range(4):
        rows = pl.ds(k * ROWS // 4, ROWS // 4)
        copies.append(pltpu.make_async_copy(a.at[rows], a_out.at[rows], sem.at[2 + k]))
    for copy in copies:
        copy.start()
    for copy in copies:
        copy.wait()


def on_device(layer_input, grad_out, w_in, w_out_t, decay_rate):
    hbm, vmem = pl.BlockSpec(memory_space=pl.ANY), pl.BlockSpec(memory_space=pltpu.VMEM)
    dma = pltpu.SemaphoreType.DMA
    buf = pltpu.VMEM
    axis_of = [ORDERS[n % 3][2] for n in range(6)]
    results = (
        jax.ShapeDtypeStruct((ROWS, WIDTH), BF16),
        jax.ShapeDtypeStruct((32, 4 * HEAD), F32),
        jax.ShapeDtypeStruct((32, HEAD), F32),
    )
    held = pl.pallas_call(
        body,
        out_shape=results,
        in_specs=[hbm, hbm, hbm, hbm, vmem],
        out_specs=(hbm, vmem, vmem),
        scratch_shapes=[
            buf((ROWS, WIDTH), BF16),
            buf((ROWS, WIDTH), BF16),
            buf((4, 2, 4, 2, 2, 32, ROWS), BF16),
            buf((4, 2, 4, 2, 2, 32, ROWS), BF16),
            buf((4, 2, 4, 2, 2, 2, 16, 5 * HEAD), BF16),
            buf((5, ROWS, HEAD), F32),
            buf((4, 2, 4, 2, 2, 16, 5 * HEAD), BF16),
            buf((4, 2, 4, 2, 2, 16, 5 * HEAD), BF16),
            buf((ROWS, 4 * HEAD), BF16),
            buf((ROWS, HALF), F32), buf((ROWS, HALF), F32), buf((ROWS, HALF), F32), buf((ROWS, HALF), F32),
            buf((ROWS, HEAD), BF16), buf((ROWS, HEAD), BF16), buf((ROWS, HEAD), BF16),
            buf((ROWS, ROWS), BF16),
            buf((HEAD // 2, HEAD), F32),
            *[buf(dims, BF16) for dims in ((HEAD, HEAD), (HEAD, HEAD), (4, HEAD // 2, HEAD), (HEAD, HEAD)) * 2],
            buf((ROWS, HEAD), BF16), buf((ROWS, HEAD), BF16),
            buf((2, ROWS, 1024), BF16),
            *[buf(BLOCK_DIMS[axis_of[n]] + inner(n), BF16) for n in range(6)],
            *[buf((2,) + BLOCK_DIMS[axis_of[n]] + inner(n), BF16) for n in range(6)],
            *[buf(PART_DIMS[axis_of[n]] + inner(n), BF16) for n in range(6)],
            *[buf((2,) + PART_DIMS[axis_of[n]] + inner(n), BF16) for n in range(6)],
            *[buf((3,) + inner(n), BF16) for n in range(6)],
            dma((6,)), dma((6, 6)),
            dma((6,)), dma((7,)), dma((6,)), dma((7,)),
            dma((1,)), dma((5,)),
            dma((5,)), dma((6, 5)),
            dma((3,)), dma((2,)),
        ],
        compiler_params=pltpu.CompilerParams(
            collective_id=0, has_side_effects=True, vmem_limit_bytes=62 * 1024 * 1024
        ),
        cost_estimate=pl.CostEstimate(flops=17 * 10**9, bytes_accessed=13 * 10**6, transcendentals=10**6),
        name="retention_backward",
    )(layer_input[0], grad_out[0], w_in.reshape(2, 16, 4 * HEAD), w_out_t.reshape(2, 16, HEAD), decay_rate[None, :])
    grad_in, grad_w, grad_wo = pl.pallas_call(
        publish, out_shape=results, in_specs=[hbm] * 3, out_specs=(hbm,) * 3, scratch_shapes=[dma((6,))], name="publish",
    )(*held)
    return grad_in[None], grad_w, grad_wo


def solution(mesh):
    rows = P(("ctx", "dp"), None)
    tokens = P("dp", "ctx", None)
    return jax.shard_map(
        on_device,
        mesh=mesh,
        in_specs=(tokens, tokens, rows, rows, P()),
        out_specs=(tokens, rows, rows),
        check_vma=False,
    )
```

time: 111 us -> 230 us (2.07)
  Pallas kernels: 104 us -> 229 us
  local copies, waits for them, and re-layouts: 6.01 us -> 0 us
    pallas_call x1 -> x2, Pallas kernels: 104 us -> 229 us  [the longest x1 133 us: on_device(): pl.pallas_call(publish, out_shape=results, in_specs=[hbm] * 3, out_specs=...]
    unnamed x7 -> x0, local copies, waits for them, and re-layouts: 6.01 us -> none
where the time goes in v2:
time: 230 us
  Pallas kernels  229 us (100%)
    pallas_call x1, Pallas kernels, on_device(): pl.pallas_call(publish, out_shape=results, in_specs=[hbm] * 3, out_specs=...  133 us
    pallas_call x1, Pallas kernels, on_device(): pl.pallas_call(body, out_shape=results, in_specs=[hbm, hbm, hbm, hbm, vme...  95.8 us

profile of v2, /device:TPU:0, one launch (start us, length us, event | category | flops | bytes accessed | tf_op | source)
XLA Modules:
  0.0 229.7 jit_solution(5848757122150696920)
XLA Ops:
  0.6 95.8 %retention_backward.1 = (bf16[512,4096]{1,0:T(8,128)(2,1)}, f32[32,1024]{1,0:T(8,128)}, f32[32,256]{1,0:T(8,128)}) custom-call(bf16[512,4096]{1,0:T(8,128)(2,1)} %bitcast.6, bf16[512,4096]{1,0:T(8,128)(2,1)} %bitcast.7, bf16[2,16,1024]{2,1,0:T(8,128)(2,1)} %bitcast.9, bf16[2,16,256]{2,1,0:T(8,128)(2,1)} %bitcast.10, f32[1,128]{1,0:T(1,128)} %bitcast.11), custom_call_target="tpu_custom_call" | custom-call | flops 16999999488 | bytes 13000000 | tf_op jit(solution)/shard_map/retention_backward/pallas_call | solution.py:496
  96.4 133.2 %publish.1 = (bf16[512,4096]{1,0:T(8,128)(2,1)}, f32[32,1024]{1,0:T(8,128)}, f32[32,256]{1,0:T(8,128)}) custom-call(bf16[512,4096]{1,0:T(8,128)(2,1)} %get-tuple-element.9.a, f32[32,1024]{1,0:T(8,128)} %get-tuple-element.10.b, f32[32,256]{1,0:T(8,128)} %get-tuple-element.11.c), custom_call_target="tpu_custom_call" | custom-call | tf_op jit(solution)/shard_map/publish/pallas_call | solution.py:535

commit v3 on v2

--- a/solution.py
+++ b/solution.py
@@ -174,14 +174,19 @@
         lax.fori_loop(0, 8, step, 0)
 
     make_tables()
-    for n in KV + QGO:
+    for n in KV:
         ag_wait(n, 0)
         ag_both(n, 1)
-    for n in KV + QGO:
+    for n in KV:
         ag_relay(n, 1)
+    for n in QGO:
+        ag_wait(n, 0)
+        ag_both(n, 1)
     for n in KV:
         ag_wait(n, 2)
         ag_both(n, 2)
+    for n in QGO:
+        ag_relay(n, 1)
     load_x.wait()
     transpose(xv, xt)
     for n in KV:
@@ -412,44 +417,44 @@
         puts.append(put)
 
     term(OUT)
+    grad_states.second()
     term(GATE)
-    grad_states.second()
     score_grad = jnp.where(before, dot(gret_ref[...], v_ref[...], 1, 1), 0.0).astype(BF16)
+    grad_states.third()
+    pair(OUT)
+    rs_first(5, 0)
     grad_q = dot(score_grad, ks_ref[...], 1, 0) + dot(gret_ref[...], state, 1, 0)
     gp[:, lanes_of(Q)] = unrotated(grad_q * twice(up_ref[...]))
     term(Q)
-    pair(OUT)
-    rs_first(5, 0)
     pair(GATE)
     rs_first(4, 0)
-    grad_states.third()
+    pr[K] = dot(score_grad, qs_ref[...], 0, 0)
+    pr[V] = dot(score_ref[...], gret_ref[...], 0, 0)
+    grad_state = (grad_states.result() * jnp.exp(-float(CENTER) * rates)).astype(BF16)
+    gp[:, lanes_of(K)] = unrotated((pr[K] + dot(v_ref[...], grad_state, 1, 0)) * twice(down_ref[...]))
+    gp[:, lanes_of(V)] = (pr[V] + dot(ks_ref[...], grad_state, 1, 1)).astype(BF16)
+    term(K)
     pair(Q)
     rs_first(3, 0)
-    grad_k = dot(score_grad, qs_ref[...], 0, 0)
+    term(V)
     rs_second(5, 0)
     rs_second(4, 0)
-    grad_state = (grad_states.result() * jnp.exp(-float(CENTER) * rates)).astype(BF16)
-    gp[:, lanes_of(K)] = unrotated((grad_k + dot(v_ref[...], grad_state, 1, 0)) * twice(down_ref[...]))
-    term(K)
+    pair(K)
     rs_second(3, 0)
-    grad_v = dot(score_ref[...], gret_ref[...], 0, 0) + dot(ks_ref[...], grad_state, 1, 1)
-    gp[:, lanes_of(V)] = grad_v.astype(BF16)
-    term(V)
-    pair(K)
     pair(V)
     for n in KV:
         rs_first(n, 0)
-    grad_input(0)
     for n in (5, 4, 3):
         rs_third(n, 0)
-    grad_input(1)
+    grad_input(0)
     for n in KV:
         rs_second(n, 0)
     for n in (5, 4, 3):
         rs_second(n, 1)
-    grad_input(2)
+    grad_input(1)
     for n in (5, 4, 3):
         rs_third(n, 1)
+    grad_input(2)
     for n in KV:
         rs_third(n, 0)
     grad_input(3)
@@ -472,15 +477,20 @@
     grad_states.sent()
 
 
-def publish(a, b, c, a_out, b_out, c_out, sem):
-    copies = [pltpu.make_async_copy(b, b_out, sem.at[0]), pltpu.make_async_copy(c, c_out, sem.at[1])]
+def publish(a, b, c, a_out, b_out, c_out, a_held, b_held, c_held, in_sem, out_sem):
+    ways = [(b, b_held, b_out), (c, c_held, c_out)]
     for k in range(4):
         rows = pl.ds(k * ROWS // 4, ROWS // 4)
-        copies.append(pltpu.make_async_copy(a.at[rows], a_out.at[rows], sem.at[2 + k]))
-    for copy in copies:
-        copy.start()
-    for copy in copies:
-        copy.wait()
+        ways.append((a.at[rows], a_held.at[rows], a_out.at[rows]))
+    loads = [pltpu.make_async_copy(src, held, in_sem.at[k]) for k, (src, held, _) in enumerate(ways)]
+    stores = [pltpu.make_async_copy(held, dst, out_sem.at[k]) for k, (_, held, dst) in enumerate(ways)]
+    for load in loads:
+        load.start()
+    for load, store in zip(loads, stores):
+        load.wait()
+        store.start()
+    for store in stores:
+        store.wait()
 
 
 def on_device(layer_input, grad_out, w_in, w_out_t, decay_rate):
@@ -533,7 +543,7 @@
         name="retention_backward",
     )(layer_input[0], grad_out[0], w_in.reshape(2, 16, 4 * HEAD), w_out_t.reshape(2, 16, HEAD), decay_rate[None, :])
     grad_in, grad_w, grad_wo = pl.pallas_call(
-        publish, out_shape=results, in_specs=[hbm] * 3, out_specs=(hbm,) * 3, scratch_shapes=[dma((6,))], name="publish",
+        publish, out_shape=results, in_specs=[hbm] * 3, out_specs=(hbm,) * 3, scratch_shapes=[*[buf(r.shape, r.dtype) for r in results], dma((6,)), dma((6,))], name="publish",
     )(*held)
     return grad_in[None], grad_w, grad_wo
 

time: 230 us -> 106 us (0.46)
  Pallas kernels: 229 us -> 105 us
    pallas_call x1, Pallas kernels: 133 us -> 3.55 us  [on_device(): pl.pallas_call(publish, out_shape=results, in_specs=[hbm] * 3, out_specs=...]
    pallas_call x1, Pallas kernels: 95.8 us -> 102 us  [on_device(): pl.pallas_call(body, out_shape=results, in_specs=[hbm, hbm, hbm, hbm, vme...]
where the time goes in v3:
time: 106 us
  Pallas kernels  105 us (99%)
    pallas_call x1, Pallas kernels, on_device(): pl.pallas_call(body, out_shape=results, in_specs=[hbm, hbm, hbm, hbm, vme...  102 us
    pallas_call x1, Pallas kernels, on_device(): pl.pallas_call(publish, out_shape=results, in_specs=[hbm] * 3, out_specs=...  3.55 us

profile of v3, /device:TPU:0, one launch (start us, length us, event | category | flops | bytes accessed | tf_op | source)
XLA Modules:
  0.0 106.1 jit_solution(7512825027143000482)
XLA Ops:
  0.6 101.8 %retention_backward.1 = (bf16[512,4096]{1,0:T(8,128)(2,1)}, f32[32,1024]{1,0:T(8,128)}, f32[32,256]{1,0:T(8,128)}) custom-call(bf16[512,4096]{1,0:T(8,128)(2,1)} %bitcast.6, bf16[512,4096]{1,0:T(8,128)(2,1)} %bitcast.7, bf16[2,16,1024]{2,1,0:T(8,128)(2,1)} %bitcast.9, bf16[2,16,256]{2,1,0:T(8,128)(2,1)} %bitcast.10, f32[1,128]{1,0:T(1,128)} %bitcast.11), custom_call_target="tpu_custom_call" | custom-call | flops 16999999488 | bytes 13000000 | tf_op jit(solution)/shard_map/retention_backward/pallas_call | solution.py:506
  102.4 3.5 %publish.1 = (bf16[512,4096]{1,0:T(8,128)(2,1)}, f32[32,1024]{1,0:T(8,128)}, f32[32,256]{1,0:T(8,128)}) custom-call(bf16[512,4096]{1,0:T(8,128)(2,1)} %get-tuple-element.9.a, f32[32,1024]{1,0:T(8,128)} %get-tuple-element.10.b, f32[32,256]{1,0:T(8,128)} %get-tuple-element.11.c), custom_call_target="tpu_custom_call" | custom-call | tf_op jit(solution)/shard_map/publish/pallas_call | solution.py:545

commit v4 on v3

--- a/solution.py
+++ b/solution.py
@@ -20,6 +20,8 @@
     (EVERY, slice(512, 768), 0), (EVERY, slice(768, 1024), 768), (EVERY, slice(1024, 1280), None),
 )
 KV, QGO = (0, 1, 2), (3, 4, 5)
+DIRECT = (1,)
+DIRECT_BACK = (1,)
 SPLIT = {"x": "y", "y": "z", "z": "y"}
 BLOCK_DIMS = {"x": (4, 4), "y": (2, 4, 2), "z": (4, 2, 2)}
 PART_DIMS = {"x": (4,), "y": (4,), "z": (2, 2)}
@@ -105,7 +107,7 @@
         rows, lanes, _ = PIECES[n]
         return wg.at[place(**fixed) + (core, rows, EVERY, lanes)]
 
-    W_BYTES = ((slice(0, 3), 0, 0, 0), (slice(0, 2), 0, EVERY, 0), (slice(0, 1), 0, EVERY, 0),
+    W_BYTES = ((slice(0, 3), 0, 0, 0), (slice(0, 3), 0, EVERY, 0), None,
                (slice(0, 2), EVERY, EVERY, EVERY), (0, EVERY, EVERY, EVERY), (EVERY, EVERY, EVERY, EVERY))
 
     def ag_send(n, step, to, **fixed):
@@ -123,7 +125,7 @@
     def ag_both(n, k):
         order = ORDERS[n % 3]
         axis, fixed = order[k], {a: here[a] for a in order[k:]}
-        for by in (1, 3):
+        for by in (1, 3, 2) if k in DIRECT else (1, 3):
             ag_send(n, 2 * k - 1, peer(axis, by), **fixed)
         if k == 2:
             ag_send(n, 5, sibling, **fixed)
@@ -133,10 +135,10 @@
         axis, fixed = order[k], {a: here[a] for a in order[k:]}
         split = order[0] if k == 1 else SPLIT[axis]
         ag_wait(n, 2 * k - 1)
-        for by, side in ((1, 0), (3, 1)):
+        for by, side in () if k in DIRECT else ((1, 0), (3, 1)):
             ag_send(n, 2 * k, peer(axis, by), half=(split, side), **{**fixed, axis: shifted(axis, 4 - by)})
         if k == 2:
-            for by in (1, 3):
+            for by in (1, 3, 2) if k in DIRECT else (1, 3):
                 ag_send(n, 5, sibling, **{**fixed, axis: shifted(axis, by)})
 
     def ag_opposite(n):
@@ -177,22 +179,18 @@
     for n in KV:
         ag_wait(n, 0)
         ag_both(n, 1)
-    for n in KV:
-        ag_relay(n, 1)
     for n in QGO:
         ag_wait(n, 0)
         ag_both(n, 1)
     for n in KV:
-        ag_wait(n, 2)
+        ag_wait(n, 1)
         ag_both(n, 2)
-    for n in QGO:
-        ag_relay(n, 1)
     load_x.wait()
     transpose(xv, xt)
     for n in KV:
         ag_relay(n, 2)
     for n in QGO:
-        ag_wait(n, 2)
+        ag_wait(n, 1)
         ag_both(n, 2)
     load_u.wait()
     transpose(uv, ut)
@@ -364,7 +362,12 @@
         return far.at[(EVERY, half) if split == "x" or (k == 0 and axis == "y") else (half,)]
 
     def rs_first(n, k):
-        axis, split, fixed, _, _ = rs_axis(n, k)
+        axis, split, fixed, _, near = rs_axis(n, k)
+        if k in DIRECT_BACK:
+            for slot, by in enumerate((1, 3, 2)):
+                src = sb.at[s_idx(n, **{**fixed, axis: shifted(axis, by)})]
+                send(src, near.at[slot], rs_s.at[2 * k + 1], rs_r.at[n, 2 * k + 1], peer(axis, by))
+            return
         far = shifted(axis, 2)
         for side, by in ((0, 1), (1, 3)):
             src = sb.at[s_idx(n, half=(split, side), **{**fixed, axis: far})]
@@ -372,6 +375,8 @@
 
     def rs_second(n, k):
         axis, split, fixed, far, near = rs_axis(n, k)
+        if k in DIRECT_BACK:
+            return
         arrived(far, rs_r.at[n, 2 * k])
         for side, by in ((0, 1), (1, 3)):
             at = s_idx(n, half=(split, side), **{**fixed, axis: shifted(axis, by)})
@@ -383,7 +388,10 @@
         axis, _, fixed, _, near = rs_axis(n, k)
         arrived(near, rs_r.at[n, 2 * k + 1])
         at = s_idx(n, **{**fixed, axis: here[axis]})
-        sb[at] = (sb[at].astype(F32) + near[0].astype(F32) + near[1].astype(F32)).astype(BF16)
+        total = sb[at].astype(F32)
+        for slot in range(near.shape[0]):
+            total += near[slot].astype(F32)
+        sb[at] = total.astype(BF16)
         if k == 0:
             rs_first(n, 1)
             return
@@ -417,62 +425,68 @@
         puts.append(put)
 
     term(OUT)
+    term(GATE)
     grad_states.second()
-    term(GATE)
     score_grad = jnp.where(before, dot(gret_ref[...], v_ref[...], 1, 1), 0.0).astype(BF16)
+    grad_q = dot(score_grad, ks_ref[...], 1, 0) + dot(gret_ref[...], state, 1, 0)
+    gp[:, lanes_of(Q)] = unrotated(grad_q * twice(up_ref[...]))
+    term(Q)
     grad_states.third()
     pair(OUT)
     rs_first(5, 0)
-    grad_q = dot(score_grad, ks_ref[...], 1, 0) + dot(gret_ref[...], state, 1, 0)
-    gp[:, lanes_of(Q)] = unrotated(grad_q * twice(up_ref[...]))
-    term(Q)
     pair(GATE)
     rs_first(4, 0)
+    pair(Q)
+    rs_first(3, 0)
     pr[K] = dot(score_grad, qs_ref[...], 0, 0)
-    pr[V] = dot(score_ref[...], gret_ref[...], 0, 0)
+    rs_second(5, 0)
+    rs_second(4, 0)
     grad_state = (grad_states.result() * jnp.exp(-float(CENTER) * rates)).astype(BF16)
     gp[:, lanes_of(K)] = unrotated((pr[K] + dot(v_ref[...], grad_state, 1, 0)) * twice(down_ref[...]))
+    term(K)
+    rs_second(3, 0)
+    pr[V] = dot(score_ref[...], gret_ref[...], 0, 0)
     gp[:, lanes_of(V)] = (pr[V] + dot(ks_ref[...], grad_state, 1, 1)).astype(BF16)
-    term(K)
-    pair(Q)
-    rs_first(3, 0)
     term(V)
-    rs_second(5, 0)
-    rs_second(4, 0)
     pair(K)
-    rs_second(3, 0)
     pair(V)
-    for n in KV:
-        rs_first(n, 0)
-    for n in (5, 4, 3):
-        rs_third(n, 0)
+    rs_first(0, 0)
+    rs_first(1, 0)
+    rs_first(2, 0)
+    rs_third(5, 0)
+    rs_third(4, 0)
+    rs_third(3, 0)
     grad_input(0)
-    for n in KV:
-        rs_second(n, 0)
-    for n in (5, 4, 3):
-        rs_second(n, 1)
+    rs_second(0, 0)
+    rs_second(1, 0)
+    rs_second(2, 0)
     grad_input(1)
-    for n in (5, 4, 3):
-        rs_third(n, 1)
+    rs_third(5, 1)
+    rs_third(4, 1)
+    rs_third(3, 1)
     grad_input(2)
-    for n in KV:
-        rs_third(n, 0)
+    rs_third(0, 0)
+    rs_third(1, 0)
+    rs_third(2, 0)
+    rs_end(5)
+    rs_end(4)
+    rs_end(3)
     grad_input(3)
-    for n in KV:
-        rs_second(n, 1)
-    for n in (5, 4, 3):
-        rs_end(n)
-    for n in KV:
-        rs_third(n, 1)
-    for n in KV:
-        rs_end(n)
+    rs_third(0, 1)
+    rs_third(1, 1)
+    rs_third(2, 1)
+    rs_end(0)
+    rs_end(1)
+    rs_end(2)
     for put in puts[2:]:
         put.wait()
     for step, of in enumerate(W_BYTES):
-        sent(wg.at[of + (0,)], ag_s.at[step])
+        if of is not None:
+            sent(wg.at[of + (0,)], ag_s.at[step])
     sent(sb, sib_s.at[0])
-    for step, of in enumerate(((0,), (slice(0, 2),), (slice(0, 1), 0, EVERY, 0), (slice(0, 2), 0, EVERY, 0), (slice(0, 3), 0, 0, 0))):
-        sent(sb.at[of], rs_s.at[step])
+    for step, of in enumerate(((0,), (slice(0, 2),), None, (slice(0, 3), 0, EVERY, 0), (slice(0, 3), 0, 0, 0))):
+        if of is not None:
+            sent(sb.at[of], rs_s.at[step])
     states.sent()
     grad_states.sent()
 
@@ -528,7 +542,7 @@
             *[buf(BLOCK_DIMS[axis_of[n]] + inner(n), BF16) for n in range(6)],
             *[buf((2,) + BLOCK_DIMS[axis_of[n]] + inner(n), BF16) for n in range(6)],
             *[buf(PART_DIMS[axis_of[n]] + inner(n), BF16) for n in range(6)],
-            *[buf((2,) + PART_DIMS[axis_of[n]] + inner(n), BF16) for n in range(6)],
+            *[buf((3,) + PART_DIMS[axis_of[n]] + inner(n), BF16) for n in range(6)],
             *[buf((3,) + inner(n), BF16) for n in range(6)],
             dma((6,)), dma((6, 6)),
             dma((6,)), dma((7,)), dma((6,)), dma((7,)),

time: 106 us -> 96.3 us (0.908)
  Pallas kernels: 105 us -> 95.4 us
    pallas_call x1, Pallas kernels: 102 us -> 91.9 us  [on_device(): pl.pallas_call(body, out_shape=results, in_specs=[hbm, hbm, hbm, hbm, vme...]
where the time goes in v4:
time: 96.3 us; the launch traced here: 96.2 us
  Pallas kernels  95.4 us (99%)
    pallas_call x1, Pallas kernels, on_device(): pl.pallas_call(body, out_shape=results, in_specs=[hbm, hbm, hbm, hbm, vme...  91.9 us
    pallas_call x1, Pallas kernels, on_device(): pl.pallas_call(publish, out_shape=results, in_specs=[hbm] * 3, out_specs=...  3.55 us

profile of v4, /device:TPU:0, one launch (start us, length us, event | category | flops | bytes accessed | tf_op | source)
XLA Modules:
  0.0 96.2 jit_solution(4954060294228995941)
XLA Ops:
  0.6 91.9 %retention_backward.1 = (bf16[512,4096]{1,0:T(8,128)(2,1)}, f32[32,1024]{1,0:T(8,128)}, f32[32,256]{1,0:T(8,128)}) custom-call(bf16[512,4096]{1,0:T(8,128)(2,1)} %bitcast.6, bf16[512,4096]{1,0:T(8,128)(2,1)} %bitcast.7, bf16[2,16,1024]{2,1,0:T(8,128)(2,1)} %bitcast.9, bf16[2,16,256]{2,1,0:T(8,128)(2,1)} %bitcast.10, f32[1,128]{1,0:T(1,128)} %bitcast.11), custom_call_target="tpu_custom_call" | custom-call | flops 16999999488 | bytes 13000000 | tf_op jit(solution)/shard_map/retention_backward/pallas_call | solution.py:520
  92.5 3.5 %publish.1 = (bf16[512,4096]{1,0:T(8,128)(2,1)}, f32[32,1024]{1,0:T(8,128)}, f32[32,256]{1,0:T(8,128)}) custom-call(bf16[512,4096]{1,0:T(8,128)(2,1)} %get-tuple-element.9.a, f32[32,1024]{1,0:T(8,128)} %get-tuple-element.10.b, f32[32,256]{1,0:T(8,128)} %get-tuple-element.11.c), custom_call_target="tpu_custom_call" | custom-call | tf_op jit(solution)/shard_map/publish/pallas_call | solution.py:559
